TPU v7x, 256 devices: a whole 4x4x8 slice. The times are simulated.
256 devices in a mesh: band: 32 (over z, x), gvec: 8 (over y, core).
Axes of the slice: x: 4, y: 4, z: 8, core: 2. Of those that a mesh axis runs over, the one named last changes fastest.
Arguments:
- pairs: bfloat16 [32, 8, 512, 640], P(None, 'gvec', 'band'), may hold values from -0.59765625 to 0.59765625
- cond_energy: float32 [512], replicated, may hold values from 0.5 to 12
- val_energy: float32 [32, 8], replicated, may hold values from -12 to -2
- band_counts: int32 [32], replicated, may hold values from 1 to 16, as said below
- slab: int32 [1], replicated, may hold values from 0 to 31
Outputs:
- chi_zero: float32 [20480, 20480], P('gvec', 'band')
Inputs may be any that keep to these rules, and one draw needn't show every extreme that they name: `band_counts`: every owner has at least one occupied slot, and in every draw some owner has all 16 slots occupied.
All inputs are finite; a program needn't handle non-finite values.
Results may differ from a plain program's by a relative error of at most 0.0028.
Values may be sent and summed in bfloat16 or wider, within the bound.
No kernel may reach another device: no remote copies, remote signals or barrier semaphores. Data moves between devices by JAX's collectives and lax.ppermute only.
A program may use at most 128 MiB of HBM per device.

v0:
```python
import jax
import jax.numpy as jnp
from jax import lax
from jax.sharding import PartitionSpec as P


def on_device(pairs, cond_energy, val_energy, band_counts, slab):
    n_band = lax.axis_size("band")
    n_gvec = lax.axis_size("gvec")
    ratio = n_band // n_gvec
    local_v = pairs.shape[1]
    slot_count = pairs.shape[2]
    col_width = pairs.shape[3]
    energies = lax.dynamic_index_in_dim(val_energy, slab[0], 0, keepdims=False)
    slots = jnp.arange(slot_count, dtype=jnp.int32)
    live = (slots[None, :] < band_counts[:, None]).reshape(-1)
    weight = jnp.where(
        live[None, :], 2.0 / (energies[:, None] - cond_energy[None, :]), jnp.float32(0.0)
    )
    blocked = pairs.reshape(n_gvec, ratio, local_v, slot_count, col_width)
    by_block = lax.all_to_all(blocked, "gvec", split_axis=0, concat_axis=2, tiled=True)
    rows_all = lax.all_gather(by_block, "band", axis=3, tiled=True)[0]
    by_column = lax.all_to_all(pairs, "band", split_axis=0, concat_axis=2, tiled=True)
    cols_all = lax.all_gather(by_column, "gvec", axis=1, tiled=True)[0]
    scaled = (weight[:, :, None] * cols_all.astype(jnp.float32)).astype(jnp.bfloat16)
    result = lax.dot_general(
        rows_all, scaled, (((1, 2), (0, 1)), ((), ())), preferred_element_type=jnp.float32
    )
    return result.reshape(ratio * col_width, col_width)


def solution(mesh):
    in_specs = (P(None, "gvec", "band", None), P(), P(), P(), P())
    out_specs = P("gvec", "band")
    return jax.shard_map(
        on_device, mesh=mesh, in_specs=in_specs, out_specs=out_specs, check_vma=False
    )
```

profile of v0, /device:TPU:1, one launch (start us, length us, event | category | flops | bytes accessed | tf_op | source)
XLA Modules:
  0.0 263.4 jit_solution(6837848196494836438)
XLA Ops:
  6.5 0.0 copy-start
  6.5 0.0 all-gather.6.cloned.1.call-start
  6.5 17.7 %all_to_all.30 = bf16[8,4,1,16,640]{4,3,2,1,0:T(8,128)(2,1)S(1)} all-to-all(bf16[8,4,1,16,640]{4,3,2,1,0:T(8,128)(2,1)} %bitcast.24), channel_id=1, replica_groups=mesh['band'=32,'gvec'=8] {'gvec'}, dimensions={0} | all-to-all | bytes 1310720 | tf_op jit(solution)/shard_map/all_to_all | solution.py:21
  24.3 1.2 copy.8
  25.5 0.0 all-gather.6.cloned.1.call-update
  25.5 0.0 all-gather.4.cloned.1.call-start
  25.6 32.6 %all_to_all.31 = bf16[32,1,16,640]{3,2,1,0:T(8,128)(2,1)} all-to-all(bf16[32,1,16,640]{3,2,1,0:T(8,128)(2,1)} %param.5), channel_id=1, replica_groups=mesh['band'=32,'gvec'=8] {'band'}, dimensions={0} | all-to-all | bytes 1310720 | tf_op jit(solution)/shard_map/all_to_all | solution.py:23
  58.2 0.0 all-gather.4.cloned.1.call-update
  58.8 0.7 iota_compare_fusion
  59.6 0.1 lt.27
  59.7 0.0 copy-done
  59.7 0.2 dynamic-slice_reduce_fusion
  59.8 0.8 divide_select_fusion
  60.6 133.8 %all-gather.6.cloned.1.call-done = bf16[1,4,8,1,512,640]{5,2,3,1,0,4:T(8,128)(2,1)} async-done(((bf16[1,4,8,1,16,640]{5,2,3,1,0,4:T(8,128)(2,1)}), bf16[1,4,8,1,512,640]{5,2,3,1,0,4:T(8,128)(2,1)}) %all-gather.6.cloned.1.call-update) | async-done | bytes 20971536 | tf_op jit(solution)/shard_map/all_gather | solution.py:22
  194.4 30.2 %copy.9 = bf16[1,4,8,1,512,640]{4,5,2,1,3,0:T(8,128)(2,1)} copy(bf16[1,4,8,1,512,640]{5,2,3,1,0,4:T(8,128)(2,1)} %all-gather.6.cloned.1.call-done) | data formatting | bytes 41943040 | tf_op jit(solution)/shard_map/all_gather | solution.py:22
  224.6 8.6 %all-gather.4.cloned.1.call-done = bf16[1,8,512,640]{3,2,0,1:T(8,128)(2,1)} async-done(((bf16[1,1,512,640]{3,2,0,1:T(8,128)(2,1)}), bf16[1,8,512,640]{3,2,0,1:T(8,128)(2,1)}) %all-gather.4.cloned.1.call-update) | async-done | bytes 5242896 | tf_op jit(solution)/shard_map/all_gather | solution.py:24
  233.3 23.3 %fusion = f32[640,4,640,1]{0,2,3,1:T(8,128)} fusion(bf16[1,4,8,1,512,640]{4,5,2,1,3,0:T(8,128)(2,1)} %copy.9, bf16[1,8,512,640]{3,2,0,1:T(8,128)(2,1)} %all-gather.4.cloned.1.call-done, f32[8,512]{1,0:T(8,128)S(1)} %divide_select_fusion), kind=kOutput, calls=%fused_computation | convolution fusion | flops 13429637120 | bytes 32784384 | tf_op jit(solution)/shard_map/dot_general | solution.py:26
Async XLA Ops:
  6.5 53.1 %copy-start = (f32[32,8]{0,1:T(8,128)S(1)}, f32[32,8]{0,1:T(8,128)}, u32[]{:S(2)}) copy-start(f32[32,8]{0,1:T(8,128)} %param.7) | copy-start | bytes 3076
  6.5 187.9 %all-gather.6.cloned.1.call-start = ((), (), s32[]{:S(2)}) async-start(), calls=%async_computation.3 | async-start | bytes 21626880 | tf_op jit(solution)/shard_map/all_gather | solution.py:22
  25.5 207.7 %all-gather.4.cloned.1.call-start = ((), (), s32[]{:S(2)}) async-start(), calls=%async_computation.2 | async-start | bytes 5898240 | tf_op jit(solution)/shard_map/all_gather | solution.py:24
Sparse Core Ops, SparseCore 0:
  25.6 168.7 all-gather.5
  196.3 36.9 all-gather.3
where the time goes:
time: 264 us; the launch traced here: 263 us
  waiting for transfers between devices  142 us (54%)
  blocking collectives  50.3 us (19%)
  local copies, waits for them, and re-layouts  31.7 us (12%)
  matrix products  23.3 us (9%)
  between operations  14.1 us (5%)
    all_gather x1, waiting for transfers between devices, on_device(): rows_all = lax.all_gather(by_block, 'band', axis=3, tiled=True)[0]  134 us
    all_to_all x1, blocking collectives, on_device(): lax.all_to_all(pairs, 'band', split_axis=0, concat_axis=2, tiled=True)  32.6 us
    all_gather x1, local copies, waits for them, and re-layouts, on_device(): rows_all = lax.all_gather(by_block, 'band', axis=3, tiled=True)[0]  30.2 us
    dot_general x1, matrix products, on_device(): lax.dot_general(rows_all, scaled, (((1, 2), (0, 1)), ((), ())), preferred...  23.3 us
    all_to_all x1, blocking collectives, on_device(): lax.all_to_all(blocked, 'gvec', split_axis=0, concat_axis=2, tiled=True)  17.7 us
    all_gather x1, waiting for transfers between devices, on_device(): cols_all = lax.all_gather(by_column, 'gvec', axis=1, tiled=True)[0]  8.62 us
  transfers between devices with their start and end apart: 2, of which 2 were waited for; matrix products, arithmetic and copies ran while one was open for 12% of the time, Pallas kernels for 0%

commit v1 on v0

--- a/solution.py
+++ b/solution.py
@@ -2,6 +2,18 @@
 import jax.numpy as jnp
 from jax import lax
 from jax.sharding import PartitionSpec as P
+
+
+def split_up(x, dim, devices):
+    shape = x.shape
+    blocks = x.reshape(*shape[:dim], devices, shape[dim] // devices, *shape[dim + 1 :])
+    return jnp.moveaxis(blocks, dim, 0)
+
+
+def joined_along(blocks, dim):
+    shape = list(blocks.shape[1:])
+    shape[dim] *= blocks.shape[0]
+    return jnp.moveaxis(blocks, 0, dim).reshape(shape)
 
 
 def on_device(pairs, cond_energy, val_energy, band_counts, slab):
@@ -18,7 +30,14 @@
         live[None, :], 2.0 / (energies[:, None] - cond_energy[None, :]), jnp.float32(0.0)
     )
     blocked = pairs.reshape(n_gvec, ratio, local_v, slot_count, col_width)
-    by_block = lax.all_to_all(blocked, "gvec", split_axis=0, concat_axis=2, tiled=True)
+    size, index = (lax.axis_size("gvec"), lax.axis_index("gvec"))
+    pieces = split_up(blocked, 0, size)
+    outs = [pieces[index]]
+    for turn in range(1, size):
+        sent = pieces[index ^ turn]
+        outs.append(lax.ppermute(sent, "gvec", [(i, i ^ turn) for i in range(size)]))
+    pieces = jnp.stack(outs)[index ^ jnp.arange(size)]
+    by_block = joined_along(pieces, 2)
     rows_all = lax.all_gather(by_block, "band", axis=3, tiled=True)[0]
     by_column = lax.all_to_all(pairs, "band", split_axis=0, concat_axis=2, tiled=True)
     cols_all = lax.all_gather(by_column, "gvec", axis=1, tiled=True)[0]

time: 264 us -> 266 us (level)
  blocking collectives: 50.3 us -> 34 us
  starting transfers between devices: 0.04 us -> 11.5 us
  waiting for transfers between devices: 142 us -> 149 us
    all_gather x1 -> x0, local copies, waits for them, and re-layouts: 30.2 us -> none  [on_device(): rows_all = lax.all_gather(by_block, 'band', axis=3, tiled=True)[0]]
    dot_general x0 -> x1, local copies, waits for them, and re-layouts: none -> 29 us  [on_device(): lax.dot_general(rows_all, scaled, (((1, 2), (0, 1)), ((), ())), preferred...]
    all_to_all x1 -> x0, blocking collectives: 17.7 us -> none  [on_device(): lax.all_to_all(blocked, 'gvec', split_axis=0, concat_axis=2, tiled=True)]
    ppermute x0 -> x7, starting transfers between devices: none -> 11.4 us  [on_device(): lax.ppermute(sent, 'gvec', [(i, i ^ turn) for i in range(size)])]
    ppermute x0 -> x7, waiting for transfers between devices: none -> 5.68 us  [on_device(): lax.ppermute(sent, 'gvec', [(i, i ^ turn) for i in range(size)])]
  transfers between devices with their start and end apart: 2 -> 9, of which waited for: 2 -> 5; matrix products, arithmetic and copies ran while one was open for 12% -> 12% of each run, Pallas kernels for 0% -> 0%
where the time goes in v1:
time: 266 us; the launch traced here: 265 us
  waiting for transfers between devices  149 us (56%)
  blocking collectives  34 us (13%)
  local copies, waits for them, and re-layouts  32.1 us (12%)
  matrix products  23.1 us (9%)
  between operations  14.1 us (5%)
  starting transfers between devices  11.5 us (4%)
    all_gather x1, waiting for transfers between devices, on_device(): rows_all = lax.all_gather(by_block, 'band', axis=3, tiled=True)[0]  133 us
    all_to_all x1, blocking collectives, on_device(): lax.all_to_all(pairs, 'band', split_axis=0, concat_axis=2, tiled=True)  34 us
    dot_general x1, local copies, waits for them, and re-layouts, on_device(): lax.dot_general(rows_all, scaled, (((1, 2), (0, 1)), ((), ())), preferred...  29 us
    dot_general x1, matrix products, on_device(): lax.dot_general(rows_all, scaled, (((1, 2), (0, 1)), ((), ())), preferred...  23.1 us
    ppermute x7, starting transfers between devices, on_device(): lax.ppermute(sent, 'gvec', [(i, i ^ turn) for i in range(size)])  11.4 us
    all_gather x1, waiting for transfers between devices, on_device(): cols_all = lax.all_gather(by_column, 'gvec', axis=1, tiled=True)[0]  9.81 us
    ppermute x7, waiting for transfers between devices, on_device(): lax.ppermute(sent, 'gvec', [(i, i ^ turn) for i in range(size)])  5.68 us
  transfers between devices with their start and end apart: 9, of which 5 were waited for; matrix products, arithmetic and copies ran while one was open for 12% of the time, Pallas kernels for 0%

profile of v1, /device:TPU:1, one launch (start us, length us, event | category | flops | bytes accessed | tf_op | source)
XLA Modules:
  0.0 264.8 jit_solution(14701912889824904717)
XLA Ops:
  6.5 0.0 copy-start
  6.5 0.0 all-gather.6.cloned.1.call-start
  6.5 1.2 dynamic-slice_bitcast_fusion
  7.8 3.3 %collective-permute-start = (bf16[1,4,1,16,640]{4,3,1,2,0:T(8,128)(2,1)S(1)}, bf16[1,4,1,16,640]{4,3,1,2,0:T(8,128)(2,1)S(1)}, u32[]{:S(2)}, u32[]{:S(2)}) collective-permute-start(bf16[1,4,1,16,640]{4,3,1,2,0:T(8,128)(2,1)S(1)} %get-tuple-element.11), channel_id=1, source_target_pairs={{0,1},{1,0},{2,3},{3,2},{4,5},{5,4},{6,7},{7,6},{8,9},{9,8},{10,11... | collective-permute-start | bytes 245768 | tf_op jit(solution)/shard_map/ppermute | solution.py:38
  11.1 0.0 collective-permute-start.1
  11.1 1.7 collective-permute-start.2
  12.8 1.2 collective-permute-start.3
  14.0 2.1 collective-permute-start.4
  16.1 0.0 collective-permute-done
  16.2 1.1 collective-permute-start.5
  17.3 0.0 collective-permute-done.1
  17.3 2.0 collective-permute-start.6
  19.3 0.0 collective-permute-done.2
  19.3 0.0 collective-permute-done.3
  19.3 2.0 collective-permute-done.4
  21.4 1.9 collective-permute-done.5
  23.3 1.7 collective-permute-done.6
  25.0 1.5 gather_fusion
  26.5 0.0 all-gather.6.cloned.1.call-update
  26.5 0.0 all-gather.4.cloned.1.call-start
  26.6 34.0 %all_to_all.12 = bf16[32,1,16,640]{3,2,1,0:T(8,128)(2,1)} all-to-all(bf16[32,1,16,640]{3,2,1,0:T(8,128)(2,1)} %param.5), channel_id=1, replica_groups=mesh['band'=32,'gvec'=8] {'band'}, dimensions={0} | all-to-all | bytes 1310720 | tf_op jit(solution)/shard_map/all_to_all | solution.py:42
  60.6 0.0 all-gather.4.cloned.1.call-update
  61.3 0.7 iota_compare_fusion
  62.0 0.1 lt.70
  62.1 0.0 copy-done
  62.1 0.2 dynamic-slice_reduce_fusion
  62.3 0.8 divide_select_fusion
  63.0 133.0 %all-gather.6.cloned.1.call-done = bf16[1,4,8,1,512,640]{5,4,1,2,3,0:T(8,128)(2,1)} async-done(((bf16[1,4,8,1,16,640]{5,4,1,2,3,0:T(8,128)(2,1)}), bf16[1,4,8,1,512,640]{5,4,1,2,3,0:T(8,128)(2,1)}) %all-gather.6.cloned.1.call-update) | async-done | bytes 20971536 | tf_op jit(solution)/shard_map/all_gather | solution.py:41
  196.0 29.0 %copy.7 = bf16[4,640,8,512]{3,1,0,2:T(8,128)(2,1)} copy(bf16[4,640,8,512]{1,3,0,2:T(8,128)(2,1)} %bitcast.50) | data formatting | bytes 41943040 | tf_op jit(solution)/shard_map/dot_general | solution.py:45
  225.1 9.8 %all-gather.4.cloned.1.call-done = bf16[1,8,512,640]{3,2,0,1:T(8,128)(2,1)} async-done(((bf16[1,1,512,640]{3,2,0,1:T(8,128)(2,1)}), bf16[1,8,512,640]{3,2,0,1:T(8,128)(2,1)}) %all-gather.4.cloned.1.call-update) | async-done | bytes 5242896 | tf_op jit(solution)/shard_map/all_gather | solution.py:43
  234.9 23.1 %convolution_bitcast_fusion = f32[2560,640]{1,0:T(8,128)} fusion(bf16[2560,8,512]{2,0,1:T(8,128)(2,1)} %bitcast.51, bf16[1,8,512,640]{3,2,0,1:T(8,128)(2,1)} %all-gather.4.cloned.1.call-done, f32[8,512]{1,0:T(8,128)S(1)} %divide_select_fusion), kind=kOutput, calls=%fused_computation.2 | convolution fusion | flops 13429637120 | bytes 32784384 | tf_op jit(solution)/shard_map/dot_general | solution.py:45
  (9 shorter events, 0.1 us)
Async XLA Ops:
  6.5 55.6 %copy-start = (f32[32,8]{0,1:T(8,128)S(1)}, f32[32,8]{0,1:T(8,128)}, u32[]{:S(2)}) copy-start(f32[32,8]{0,1:T(8,128)} %param.7) | copy-start | bytes 3076
  6.5 189.5 %all-gather.6.cloned.1.call-start = ((), (), s32[]{:S(2)}) async-start(), calls=%async_computation.2 | async-start | bytes 21626880 | tf_op jit(solution)/shard_map/all_gather | solution.py:41
  7.8 8.4 %collective-permute-start = (bf16[1,4,1,16,640]{4,3,1,2,0:T(8,128)(2,1)S(1)}, bf16[1,4,1,16,640]{4,3,1,2,0:T(8,128)(2,1)S(1)}, u32[]{:S(2)}, u32[]{:S(2)}) collective-permute-start(bf16[1,4,1,16,640]{4,3,1,2,0:T(8,128)(2,1)S(1)} %get-tuple-element.11), channel_id=1, source_target_pairs={{0,1},{1,0},{2,3},{3,2},{4,5},{5,4},{6,7},{7,6},{8,9},{9,8},{10,11... | collective-permute-start | bytes 245768 | tf_op jit(solution)/shard_map/ppermute | solution.py:38
  11.1 6.2 %collective-permute-start.1 = (bf16[1,4,1,16,640]{4,3,1,2,0:T(8,128)(2,1)S(1)}, bf16[1,4,1,16,640]{4,3,1,2,0:T(8,128)(2,1)S(1)}, u32[]{:S(2)}, u32[]{:S(2)}) collective-permute-start(bf16[1,4,1,16,640]{4,3,1,2,0:T(8,128)(2,1)S(1)} %get-tuple-element.10), channel_id=1, source_target_pairs={{0,2},{1,3},{2,0},{3,1},{4,6},{5,7},{6,4},{7,5},{8,10},{9,11},{10,... | collective-permute-start | bytes 245768 | tf_op jit(solution)/shard_map/ppermute | solution.py:38
  11.1 8.2 %collective-permute-start.2 = (bf16[1,4,1,16,640]{4,3,1,2,0:T(8,128)(2,1)S(1)}, bf16[1,4,1,16,640]{4,3,1,2,0:T(8,128)(2,1)S(1)}, u32[]{:S(2)}, u32[]{:S(2)}) collective-permute-start(bf16[1,4,1,16,640]{4,3,1,2,0:T(8,128)(2,1)S(1)} %get-tuple-element.9), channel_id=1, source_target_pairs={{0,3},{1,2},{2,1},{3,0},{4,7},{5,6},{6,5},{7,4},{8,11},{9,10},{10,... | collective-permute-start | bytes 245768 | tf_op jit(solution)/shard_map/ppermute | solution.py:38
  12.8 6.5 %collective-permute-start.3 = (bf16[1,4,1,16,640]{4,3,1,2,0:T(8,128)(2,1)S(1)}, bf16[1,4,1,16,640]{4,3,1,2,0:T(8,128)(2,1)S(1)}, u32[]{:S(2)}, u32[]{:S(2)}) collective-permute-start(bf16[1,4,1,16,640]{4,3,1,2,0:T(8,128)(2,1)S(1)} %get-tuple-element.8), channel_id=1, source_target_pairs={{0,4},{1,5},{2,6},{3,7},{4,0},{5,1},{6,2},{7,3},{8,12},{9,13},{10,... | collective-permute-start | bytes 245768 | tf_op jit(solution)/shard_map/ppermute | solution.py:38
  14.0 7.4 %collective-permute-start.4 = (bf16[1,4,1,16,640]{4,3,1,2,0:T(8,128)(2,1)S(1)}, bf16[1,4,1,16,640]{4,3,1,2,0:T(8,128)(2,1)S(1)}, u32[]{:S(2)}, u32[]{:S(2)}) collective-permute-start(bf16[1,4,1,16,640]{4,3,1,2,0:T(8,128)(2,1)S(1)} %get-tuple-element.7), channel_id=1, source_target_pairs={{0,5},{1,4},{2,7},{3,6},{4,1},{5,0},{6,3},{7,2},{8,13},{9,12},{10,... | collective-permute-start | bytes 245768 | tf_op jit(solution)/shard_map/ppermute | solution.py:38
  16.2 7.1 %collective-permute-start.5 = (bf16[1,4,1,16,640]{4,3,1,2,0:T(8,128)(2,1)S(1)}, bf16[1,4,1,16,640]{4,3,1,2,0:T(8,128)(2,1)S(1)}, u32[]{:S(2)}, u32[]{:S(2)}) collective-permute-start(bf16[1,4,1,16,640]{4,3,1,2,0:T(8,128)(2,1)S(1)} %get-tuple-element.6), channel_id=1, source_target_pairs={{0,6},{1,7},{2,4},{3,5},{4,2},{5,3},{6,0},{7,1},{8,14},{9,15},{10,... | collective-permute-start | bytes 245768 | tf_op jit(solution)/shard_map/ppermute | solution.py:38
  17.3 7.8 %collective-permute-start.6 = (bf16[1,4,1,16,640]{4,3,1,2,0:T(8,128)(2,1)S(1)}, bf16[1,4,1,16,640]{4,3,1,2,0:T(8,128)(2,1)S(1)}, u32[]{:S(2)}, u32[]{:S(2)}) collective-permute-start(bf16[1,4,1,16,640]{4,3,1,2,0:T(8,128)(2,1)S(1)} %get-tuple-element.5), channel_id=1, source_target_pairs={{0,7},{1,6},{2,5},{3,4},{4,3},{5,2},{6,1},{7,0},{8,15},{9,14},{10,... | collective-permute-start | bytes 245768 | tf_op jit(solution)/shard_map/ppermute | solution.py:38
  26.5 208.3 %all-gather.4.cloned.1.call-start = ((), (), s32[]{:S(2)}) async-start(), calls=%async_computation.1 | async-start | bytes 5898240 | tf_op jit(solution)/shard_map/all_gather | solution.py:43
Sparse Core Ops, SparseCore 0:
  26.7 169.3 all-gather.5
  197.9 36.9 all-gather.3
